TPU v7x, 32 devices: a whole 2x2x4 slice. The times are simulated.
32 devices in a mesh: section: 4 (over x, core), space: 8 (over z, y).
Axes of the slice: x: 2, y: 2, z: 4, core: 2. Of those that a mesh axis runs over, the one named last changes fastest.
Arguments:
- frames: bfloat16 [4, 4, 128, 96, 128], P('section', None, 'space'), may hold values from -6 to 6
- patch_weight: bfloat16 [2, 256, 128], replicated, may hold values from -0.25 to 0.25
- patch_bias: float32 [128], replicated, may hold values from -3 to 3
- enc_weight: bfloat16 [1152, 128], replicated, may hold values from -0.1875 to 0.1875
- cell_weight: bfloat16 [4, 2304, 512], P('section'), may hold values from -0.125 to 1.25
- cell_bias: float32 [4, 512], P('section'), may hold values from -3 to 4
- head_weight: bfloat16 [3, 1152, 128], replicated, may hold values from -0.1875 to 0.1875
- out_weight: bfloat16 [128, 512], replicated, may hold values from -0.5 to 0.5
- out_bias: float32 [512], replicated, may hold values from -2 to 2
Outputs:
- logits: bfloat16 [4, 4, 64, 48, 512], P('section', None, 'space')
All inputs are finite; a program needn't handle non-finite values.
Results may differ from a plain program's by a relative error of at most 0.015.
Values may be sent and summed in bfloat16 or wider, within the bound.
A program may use at most 64 MiB of HBM per device.

v0:
```python
import functools

import jax
import jax.numpy as jnp
from jax import lax
from jax.experimental import pallas as pl
from jax.experimental.pallas import tpu as pltpu
from jax.sharding import PartitionSpec as P

MESH = pl.DeviceIdType.MESH
BF16 = jnp.bfloat16
F32 = jnp.float32


def sigmoid(x):
    return 0.5 * jnp.tanh(0.5 * x) + 0.5


def shifted(field, by):
    cols = field.shape[1]
    wide = field.astype(F32)
    col = lax.broadcasted_iota(jnp.int32, field.shape, 1)
    left = jnp.where(col >= by, pltpu.roll(wide, by, 1), 0.0).astype(BF16)
    right = jnp.where(col < cols - by, pltpu.roll(wide, cols - by, 1), 0.0).astype(BF16)
    return left, field, right


def kernel(
    sections, spaces,
    frames, pw, pb, ew, cw_hbm, cb, hw,
    out,
    fr, cw, proj, ebox, enc, xbox, hbox, gbox, l1box, l2box, mem, resid, joined,
    fr_sem, cw_sem, e_recv, e_send, enc_send, x_recv, h_recv, u_send, g_recv,
    l1_recv, l1_send, l2_recv, l2_send,
):
    layer = lax.axis_index("section")
    place = lax.axis_index("space")
    last = sections - 1
    has_up = place > 0
    has_down = place < spaces - 1
    above = jnp.maximum(place - 1, 0)
    below = jnp.minimum(place + 1, spaces - 1)
    onward = jnp.minimum(layer + 1, last)
    steps, rows = fr.shape[0], fr.shape[1]
    cols, ch = proj.shape[1] // rows, proj.shape[2]
    cells = rows * cols

    def frame_copy(t):
        return pltpu.make_async_copy(frames.at[t], fr.at[t], fr_sem.at[t])

    weight_copy = pltpu.make_async_copy(cw_hbm, cw, cw_sem.at[0])
    for t in range(steps):
        frame_copy(t).start()
    weight_copy.start()

    barrier = pltpu.get_barrier_semaphore()
    for sec in range(sections):
        @pl.when(has_up)
        def _():
            pl.semaphore_signal(barrier, inc=1, device_id=(sec, above), device_id_type=MESH)

        @pl.when(has_down)
        def _():
            pl.semaphore_signal(barrier, inc=1, device_id=(sec, below), device_id_type=MESH)

        @pl.when(layer != sec)
        def _():
            pl.semaphore_signal(barrier, inc=1, device_id=(sec, place), device_id_type=MESH)

    @pl.when(jnp.logical_not(has_up))
    def _():
        for box, depth in ((ebox, 1), (xbox, 1), (hbox, 1), (gbox, 1), (l1box, 2), (l2box, 4)):
            box[:, 0:depth] = jnp.zeros((box.shape[0], depth, cols, ch), BF16)

    @pl.when(jnp.logical_not(has_down))
    def _():
        for box, depth in ((ebox, 1), (xbox, 1), (hbox, 1), (gbox, 1), (l1box, 2), (l2box, 4)):
            end = box.shape[1]
            box[:, end - depth:end] = jnp.zeros((box.shape[0], depth, cols, ch), BF16)

    def send(src, dst, s_sem, r_sem, sec, at):
        return pltpu.make_async_remote_copy(
            src_ref=src, dst_ref=dst, send_sem=s_sem, recv_sem=r_sem,
            device_id=(sec, at), device_id_type=MESH,
        )

    def edges(src, first, dst, depth, s_sem, s_at, r_sem, r_at, sec, go):
        end = dst.shape[0]
        up = send(src.at[pl.ds(first, depth)], dst.at[pl.ds(end - depth, depth)],
                  s_sem(s_at), r_sem(r_at + 1), sec, above)
        down = send(src.at[pl.ds(first + rows - depth, depth)], dst.at[pl.ds(0, depth)],
                    s_sem(s_at + 1), r_sem(r_at), sec, below)

        @pl.when(has_up)
        def _():
            go(up)

        @pl.when(has_down)
        def _():
            go(down)

    def start(copy):
        copy.start()

    def wait_sent(copy):
        copy.wait_send()

    def arrived(ref, sem):
        pltpu.make_async_copy(ref, ref, sem).wait()

    def edges_arrived(box, depth, sem, at):
        end = box.shape[0]

        @pl.when(has_up)
        def _():
            arrived(box.at[pl.ds(0, depth)], sem(at))

        @pl.when(has_down)
        def _():
            arrived(box.at[pl.ds(end - depth, depth)], sem(at + 1))

    def patch(a, b):
        return pw[a, b * ch:(b + 1) * ch, :]

    def ebox_edges(t, go):
        edges(ebox.at[t], 1, ebox.at[t], 1, lambda k: e_send.at[t, k], 0,
              lambda k: e_recv.at[t, k], 0, layer, go)

    def project(t):
        frame_copy(t).wait()
        fine = fr.shape[3]
        place_row = lax.broadcasted_iota(jnp.int32, (fine, fine), 0)
        place_col = lax.broadcasted_iota(jnp.int32, (fine, fine), 1)
        wanted = jnp.where(place_row < cols, 2 * place_row, 2 * place_row - (fine - 1))
        pick = jnp.where(place_col == wanted, 1.0, 0.0).astype(BF16)
        split = []
        for r in range(rows):
            pair = jnp.concatenate([fr[t, r, 0], fr[t, r, 1]], -1)
            both = jnp.dot(pick, pair, preferred_element_type=F32).astype(BF16)
            split.append(jnp.concatenate([both[:cols], both[cols:]], -1))
        weight = jnp.concatenate([patch(a, b) for b in range(2) for a in range(2)], 0)
        total = jnp.dot(jnp.concatenate(split, 0), weight, preferred_element_type=F32) + pb[...]
        rounded = total.astype(BF16)
        proj[t] = rounded
        ebox[t, pl.ds(1, rows)] = jnp.maximum(rounded, jnp.zeros((), BF16)).reshape(rows, cols, ch)

    project(0)
    present = 1 + jnp.where(has_up, 1, 0) + jnp.where(has_down, 1, 0)
    pl.semaphore_wait(barrier, sections * present - 1)
    ebox_edges(0, start)

    @pl.loop(1, steps)
    def _(t):
        project(t)
        ebox_edges(t, start)

    def conv(field, weight, by):
        parts = shifted(field, by)
        lhs = jnp.concatenate(
            [part[i * by:i * by + rows].reshape(cells, ch) for i in range(3) for part in parts], -1
        )
        return jnp.dot(lhs, weight, preferred_element_type=F32)

    def enc_out(t, go):
        slot = t * sections + layer
        edges(enc.at[t], 0, xbox.at[slot], 1, lambda k: enc_send.at[t, k], 0,
              lambda k: x_recv.at[slot, k], 0, 0, go)

    def enc_main(t):
        slot = t * sections + layer
        return send(enc.at[t], xbox.at[slot, pl.ds(1, rows)], enc_send.at[t, 2], x_recv.at[slot, 2], 0, place)

    @pl.loop(0, steps)
    def _(t):
        edges_arrived(ebox.at[t], 1, lambda k: e_recv.at[t, k], 0)
        result = proj[t].astype(F32) + conv(ebox[t], ew[...], 1)
        enc[t] = result.astype(BF16).reshape(rows, cols, ch)
        slot = t * sections + layer

        @pl.when(layer == 0)
        def _():
            pltpu.make_async_copy(enc.at[t], xbox.at[slot, pl.ds(1, rows)], x_recv.at[slot, 2]).start()

        @pl.when(layer != 0)
        def _():
            enc_main(t).start()

        enc_out(t, start)

    weight_copy.wait()

    def h_edges(slot, go):
        edges(hbox.at[slot], 1, hbox.at[slot], 1, lambda k: u_send.at[slot, k], 0,
              lambda k: h_recv.at[slot, k], 0, layer, go)

    def x_edges(slot, go):
        edges(hbox.at[slot], 1, xbox.at[slot], 1, lambda k: u_send.at[slot, k], 2,
              lambda k: x_recv.at[slot, k], 0, onward, go)

    def g_edges(t, m, go):
        slot = t * sections + m
        edges(hbox.at[slot], 1, gbox.at[t], 1, lambda k: u_send.at[slot, k], 2,
              lambda k: g_recv.at[t, k], 0, m, go)

    def x_main(slot):
        return send(hbox.at[slot, pl.ds(1, rows)], xbox.at[slot, pl.ds(1, rows)],
                    u_send.at[slot, 4], x_recv.at[slot, 2], onward, place)

    def g_main(t, m):
        slot = t * sections + m
        return send(hbox.at[slot, pl.ds(1, rows)], gbox.at[t, pl.ds(1, rows)],
                    u_send.at[slot, 4], g_recv.at[t, 2], m, place)

    def outgoing(t, m, go):
        slot = t * sections + m

        @pl.when(layer < last)
        def _():
            go(x_main(slot))
            x_edges(slot, go)

        @pl.when(layer == last)
        def _():
            @pl.when(m != last)
            def _():
                go(g_main(t, m))

            g_edges(t, m, go)

        @pl.when(t < steps - 1)
        def _():
            h_edges(slot, go)

    def unit(t, m, first):
        slot = t * sections + m
        arrived(xbox.at[slot, pl.ds(1, rows)], x_recv.at[slot, 2])
        edges_arrived(xbox.at[slot], 1, lambda k: x_recv.at[slot, k], 0)
        width = 2 * ch
        if first:
            parts = shifted(xbox[slot], 1)
            for j in range(3):
                joined[:, :, j * ch:(j + 1) * ch] = parts[j]
            lhs = jnp.concatenate(
                [joined[i:i + rows, :, 0:3 * ch].reshape(cells, 3 * ch) for i in range(3)], -1
            )
            weight = jnp.concatenate([cw[k * width:k * width + ch] for k in range(9)], 0)
        else:
            before = slot - sections
            edges_arrived(hbox.at[before], 1, lambda k: h_recv.at[before, k], 0)
            parts = shifted(xbox[slot], 1)
            for j in range(3):
                joined[:, :, j * width:j * width + ch] = parts[j]
            parts = shifted(hbox[before], 1)
            for j in range(3):
                joined[:, :, j * width + ch:(j + 1) * width] = parts[j]
            lhs = jnp.concatenate(
                [joined[i:i + rows].reshape(cells, 3 * width) for i in range(3)], -1
            )
            weight = cw[...]
        z = jnp.dot(lhs, weight, preferred_element_type=F32) + cb[...]
        new = sigmoid(z[:, :ch]) * jnp.tanh(z[:, 2 * ch:3 * ch])
        if not first:
            new = new + sigmoid(z[:, ch:2 * ch]) * mem[m]
        mem[m] = new
        hidden = (sigmoid(z[:, 3 * ch:]) * jnp.tanh(new)).astype(BF16)
        hbox[slot, pl.ds(1, rows)] = hidden.reshape(rows, cols, ch)

        @pl.when(jnp.logical_and(layer == last, m == last))
        def _():
            pltpu.make_async_copy(
                hbox.at[slot, pl.ds(1, rows)], gbox.at[t, pl.ds(1, rows)], g_recv.at[t, 2]
            ).start()

        outgoing(t, m, start)

    @pl.loop(0, sections)
    def _(m):
        unit(0, m, True)

    @pl.loop(1, steps)
    def _(t):
        @pl.loop(0, sections)
        def _(m):
            unit(t, m, False)

    def l1_edges(t, go):
        edges(l1box.at[t], 2, l1box.at[t], 2, lambda k: l1_send.at[t, k], 0,
              lambda k: l1_recv.at[t, k], 0, layer, go)

    def l2_edges(t, go):
        edges(l2box.at[t], 4, l2box.at[t], 4, lambda k: l2_send.at[t, k], 0,
              lambda k: l2_recv.at[t, k], 0, layer, go)

    zero = jnp.zeros((), BF16)

    @pl.loop(0, steps)
    def _(t):
        arrived(gbox.at[t, pl.ds(1, rows)], g_recv.at[t, 2])
        edges_arrived(gbox.at[t], 1, lambda k: g_recv.at[t, k], 0)
        base = gbox[t, pl.ds(1, rows)].reshape(cells, ch).astype(F32)
        y = base + conv(jnp.maximum(gbox[t], zero), hw[0], 1)
        resid[t] = y
        l1box[t, pl.ds(2, rows)] = jnp.maximum(y, 0.0).astype(BF16).reshape(rows, cols, ch)
        l1_edges(t, start)

    @pl.loop(0, steps)
    def _(t):
        edges_arrived(l1box.at[t], 2, lambda k: l1_recv.at[t, k], 0)
        y = resid[t] + conv(l1box[t], hw[1], 2)
        resid[t] = y
        l2box[t, pl.ds(4, rows)] = jnp.maximum(y, 0.0).astype(BF16).reshape(rows, cols, ch)
        l2_edges(t, start)

    @pl.loop(0, steps)
    def _(t):
        edges_arrived(l2box.at[t], 4, lambda k: l2_recv.at[t, k], 0)
        out[t] = (resid[t] + conv(l2box[t], hw[2], 4)).astype(BF16)

    @pl.loop(0, steps)
    def _(t):
        ebox_edges(t, wait_sent)
        enc_out(t, wait_sent)

        @pl.when(layer != 0)
        def _():
            enc_main(t).wait_send()

        l1_edges(t, wait_sent)
        l2_edges(t, wait_sent)

    @pl.loop(0, steps)
    def _(t):
        @pl.loop(0, sections)
        def _(m):
            outgoing(t, m, wait_sent)


def local(sections, spaces, frames, patch_weight, patch_bias, enc_weight, cell_weight,
          cell_bias, head_weight, out_weight, out_bias):
    _, steps, fine_rows, fine_cols, ch_in = frames.shape
    rows, cols = fine_rows // 2, fine_cols // 2
    ch = enc_weight.shape[1]
    cells = rows * cols
    slots = steps * sections
    vmem = pl.BlockSpec(memory_space=pltpu.VMEM)
    hbm = pl.BlockSpec(memory_space=pl.ANY)
    dma = pltpu.SemaphoreType.DMA
    rounded = pl.pallas_call(
        functools.partial(kernel, sections, spaces),
        out_shape=jax.ShapeDtypeStruct((steps, cells, ch), BF16),
        in_specs=[hbm, vmem, vmem, vmem, hbm, vmem, vmem],
        out_specs=vmem,
        scratch_shapes=[
            pltpu.VMEM((steps, rows, 2, fine_cols, ch_in), BF16),
            pltpu.VMEM(cell_weight.shape[1:], BF16),
            pltpu.VMEM((steps, cells, ch), BF16),
            pltpu.VMEM((steps, rows + 2, cols, ch), BF16),
            pltpu.VMEM((steps, rows, cols, ch), BF16),
            pltpu.VMEM((slots, rows + 2, cols, ch), BF16),
            pltpu.VMEM((slots, rows + 2, cols, ch), BF16),
            pltpu.VMEM((steps, rows + 2, cols, ch), BF16),
            pltpu.VMEM((steps, rows + 4, cols, ch), BF16),
            pltpu.VMEM((steps, rows + 8, cols, ch), BF16),
            pltpu.VMEM((sections, cells, ch), F32),
            pltpu.VMEM((steps, cells, ch), F32),
            pltpu.VMEM((rows + 2, cols, 6 * ch), BF16),
            dma((steps,)), dma((1,)),
            dma((steps, 2)), dma((steps, 2)), dma((steps, 3)),
            dma((slots, 3)), dma((slots, 2)), dma((slots, 5)), dma((steps, 3)),
            dma((steps, 2)), dma((steps, 2)), dma((steps, 2)), dma((steps, 2)),
        ],
        compiler_params=pltpu.CompilerParams(
            collective_id=0, has_side_effects=True, vmem_limit_bytes=48 * 1024 * 1024
        ),
        name="nowcast",
    )(
        frames.reshape(steps, rows, 2, fine_cols, ch_in),
        patch_weight,
        patch_bias.reshape(1, ch),
        enc_weight,
        cell_weight[0],
        cell_bias,
        head_weight,
    )
    logits = jnp.dot(rounded.reshape(steps * cells, ch), out_weight, preferred_element_type=F32)
    logits = (logits + out_bias).astype(BF16)
    return logits.reshape(1, steps, rows, cols, out_weight.shape[1])


def solution(mesh):
    placed = (
        P("section", None, "space", None, None),
        P(), P(), P(),
        P("section", None, None),
        P("section", None),
        P(), P(), P(),
    )
    return jax.shard_map(
        functools.partial(local, mesh.shape["section"], mesh.shape["space"]),
        mesh=mesh,
        in_specs=placed,
        out_specs=P("section", None, "space", None, None),
        check_vma=False,
    )
```

profile of v0, /device:TPU:11, one launch (start us, length us, event | category | flops | bytes accessed | tf_op | source)
XLA Modules:
  0.0 70.8 jit_solution(17402764927363194918)
XLA Ops:
  0.0 0.0 copy-start
  0.0 0.0 copy-start.1
  0.0 1.7 %copy-done.1 = bf16[1,2304,512]{2,1,0:T(8,128)(2,1)S(1)} copy-done((bf16[1,2304,512]{2,1,0:T(8,128)(2,1)S(1)}, bf16[1,2304,512]{2,1,0:T(8,128)(2,1)}, u32[]{:S(2)}) %copy-start.1) | copy-done | bytes 2359320
  1.7 0.0 copy-start.2
  1.7 1.4 %copy-done.2 = bf16[1,4,16,96,128]{4,3,2,1,0:T(8,128)(2,1)S(1)} copy-done((bf16[1,4,16,96,128]{4,3,2,1,0:T(8,128)(2,1)S(1)}, bf16[1,4,16,96,128]{4,3,2,1,0:T(8,128)(2,1)}, u32[]{:S(2)}) %copy-start.2) | copy-done | bytes 1572888
  3.1 0.0 copy-start.3
  3.1 1.2 %copy-done.3 = bf16[3,1152,128]{2,1,0:T(8,128)(2,1)S(1)} copy-done((bf16[3,1152,128]{2,1,0:T(8,128)(2,1)S(1)}, bf16[3,1152,128]{2,1,0:T(8,128)(2,1)}, u32[]{:S(2)}) %copy-start.3) | copy-done | bytes 884760
  4.3 0.0 copy-start.4
  4.3 1.0 %copy-done.4 = bf16[1152,128]{1,0:T(8,128)(2,1)S(1)} copy-done((bf16[1152,128]{1,0:T(8,128)(2,1)S(1)}, bf16[1152,128]{1,0:T(8,128)(2,1)}, u32[]{:S(2)}) %copy-start.4) | copy-done | bytes 294936
  5.2 0.0 copy-start.5
  5.2 0.9 %copy-done.5 = bf16[2,256,128]{2,1,0:T(8,128)(2,1)S(1)} copy-done((bf16[2,256,128]{2,1,0:T(8,128)(2,1)S(1)}, bf16[2,256,128]{2,1,0:T(8,128)(2,1)}, u32[]{:S(2)}) %copy-start.5) | copy-done | bytes 131096
  6.1 0.0 copy-start.6
  6.2 0.7 copy-done.6
  6.8 0.0 copy-start.7
  6.8 0.7 copy-done.7
  7.5 0.0 copy-start.8
  7.5 61.6 %nowcast.1 = bf16[4,384,128]{2,1,0:T(8,128)(2,1)S(1)} custom-call(bf16[4,8,2,96,128]{4,3,2,1,0:T(8,128)(2,1)S(1)} %bitcast.8, bf16[2,256,128]{2,1,0:T(8,128)(2,1)S(1)} %copy-done.5, f32[1,128]{1,0:T(1,128)S(1)} %bitcast.10, bf16[1152,128]{1,0:T(8,128)(2,1)S(1)} %copy-done.4, bf16[2304,512]{1,0:T(8,128)(2,1)S(1)} %bitcast.7, f32[1,512]{1,0:T(1,128)S(1)} %copy-done.6, ...), custom_call_target="tpu_custom_call" | custom-call | tf_op jit(solution)/shard_map/nowcast/pallas_call | solution.py:348
  69.1 0.0 copy-done
  69.1 0.0 copy-done.8
  69.1 1.7 %fusion = bf16[1536,512]{1,0:T(8,128)(2,1)} fusion(bf16[1536,128]{1,0:T(8,128)(2,1)S(1)} %bitcast.9, bf16[128,512]{1,0:T(8,128)(2,1)S(1)} %copy-done, f32[512]{0:T(512)S(1)} %copy-done.8), kind=kOutput, calls=%fused_computation.1 | convolution fusion | flops 202899456 | bytes 2099200 | tf_op jit(solution)/shard_map/dot_general | solution.py:385
Async XLA Ops:
  0.0 69.1 %copy-start = (bf16[128,512]{1,0:T(8,128)(2,1)S(1)}, bf16[128,512]{1,0:T(8,128)(2,1)}, u32[]{:S(2)}) copy-start(bf16[128,512]{1,0:T(8,128)(2,1)} %param.16) | copy-start | bytes 393220
  0.0 1.7 %copy-start.1 = (bf16[1,2304,512]{2,1,0:T(8,128)(2,1)S(1)}, bf16[1,2304,512]{2,1,0:T(8,128)(2,1)}, u32[]{:S(2)}) copy-start(bf16[1,2304,512]{2,1,0:T(8,128)(2,1)} %param.13) | copy-start | bytes 7077892
  1.7 1.4 %copy-start.2 = (bf16[1,4,16,96,128]{4,3,2,1,0:T(8,128)(2,1)S(1)}, bf16[1,4,16,96,128]{4,3,2,1,0:T(8,128)(2,1)}, u32[]{:S(2)}) copy-start(bf16[1,4,16,96,128]{4,3,2,1,0:T(8,128)(2,1)} %param.9) | copy-start | bytes 4718596
  3.1 1.2 %copy-start.3 = (bf16[3,1152,128]{2,1,0:T(8,128)(2,1)S(1)}, bf16[3,1152,128]{2,1,0:T(8,128)(2,1)}, u32[]{:S(2)}) copy-start(bf16[3,1152,128]{2,1,0:T(8,128)(2,1)} %hw.1) | copy-start | bytes 2654212
  4.3 1.0 %copy-start.4 = (bf16[1152,128]{1,0:T(8,128)(2,1)S(1)}, bf16[1152,128]{1,0:T(8,128)(2,1)}, u32[]{:S(2)}) copy-start(bf16[1152,128]{1,0:T(8,128)(2,1)} %ew.1) | copy-start | bytes 884740
  5.2 0.9 %copy-start.5 = (bf16[2,256,128]{2,1,0:T(8,128)(2,1)S(1)}, bf16[2,256,128]{2,1,0:T(8,128)(2,1)}, u32[]{:S(2)}) copy-start(bf16[2,256,128]{2,1,0:T(8,128)(2,1)} %pw.1) | copy-start | bytes 393220
  6.1 0.7 copy-start.6
  6.8 0.7 copy-start.7
  7.5 61.6 %copy-start.8 = (f32[512]{0:T(512)S(1)}, f32[512]{0:T(512)}, u32[]{:S(2)}) copy-start(f32[512]{0:T(512)} %param.17) | copy-start | bytes 6148
where the time goes:
time: 71.1 us; the launch traced here: 70.8 us
  Pallas kernels  61.6 us (87%)
  local copies, waits for them, and re-layouts  7.48 us (11%)
  matrix products  1.7 us (2%)
    pallas_call x1, Pallas kernels, local(): pl.pallas_call(functools.partial(kernel, sections, spaces), out_shape=jax...  61.6 us
    unnamed x18, local copies, waits for them, and re-layouts  7.48 us
    dot_general x1, matrix products, local(): jnp.dot(rounded.reshape(steps * cells, ch), out_weight, preferred_element...  1.7 us

commit v1 on v0

--- a/solution.py
+++ b/solution.py
@@ -27,10 +27,10 @@
 
 def kernel(
     sections, spaces,
-    frames, pw, pb, ew, cw_hbm, cb, hw,
-    out,
-    fr, cw, proj, ebox, enc, xbox, hbox, gbox, l1box, l2box, mem, resid, joined,
-    fr_sem, cw_sem, e_recv, e_send, enc_send, x_recv, h_recv, u_send, g_recv,
+    frames, pw_hbm, pb_hbm, ew_hbm, cw_hbm, cb_hbm, hw_hbm,
+    out_hbm,
+    fr, pw, pb, ew, cw, cb, hw, out, proj, ebox, enc, xbox, hbox, gbox, l1box, l2box, mem, resid, joined,
+    fr_sem, w_sem, out_sem, e_recv, e_send, enc_send, x_recv, h_recv, u_send, g_recv,
     l1_recv, l1_send, l2_recv, l2_send,
 ):
     layer = lax.axis_index("section")
@@ -48,10 +48,16 @@
     def frame_copy(t):
         return pltpu.make_async_copy(frames.at[t], fr.at[t], fr_sem.at[t])
 
-    weight_copy = pltpu.make_async_copy(cw_hbm, cw, cw_sem.at[0])
+    pairs = ((pw_hbm, pw), (pb_hbm, pb), (ew_hbm, ew), (cw_hbm, cw), (cb_hbm, cb), (hw_hbm, hw))
+    load_pw, load_pb, load_ew, load_cw, load_cb, load_hw = [
+        pltpu.make_async_copy(src, dst, w_sem.at[k]) for k, (src, dst) in enumerate(pairs)
+    ]
+    load_pw.start()
+    load_pb.start()
     for t in range(steps):
         frame_copy(t).start()
-    weight_copy.start()
+    for load in (load_ew, load_cw, load_cb, load_hw):
+        load.start()
 
     barrier = pltpu.get_barrier_semaphore()
     for sec in range(sections):
@@ -144,6 +150,8 @@
         proj[t] = rounded
         ebox[t, pl.ds(1, rows)] = jnp.maximum(rounded, jnp.zeros((), BF16)).reshape(rows, cols, ch)
 
+    load_pw.wait()
+    load_pb.wait()
     project(0)
     present = 1 + jnp.where(has_up, 1, 0) + jnp.where(has_down, 1, 0)
     pl.semaphore_wait(barrier, sections * present - 1)
@@ -161,6 +169,8 @@
         )
         return jnp.dot(lhs, weight, preferred_element_type=F32)
 
+    load_ew.wait()
+
     def enc_out(t, go):
         slot = t * sections + layer
         edges(enc.at[t], 0, xbox.at[slot], 1, lambda k: enc_send.at[t, k], 0,
@@ -187,7 +197,8 @@
 
         enc_out(t, start)
 
-    weight_copy.wait()
+    load_cw.wait()
+    load_cb.wait()
 
     def h_edges(slot, go):
         edges(hbox.at[slot], 1, hbox.at[slot], 1, lambda k: u_send.at[slot, k], 0,
@@ -283,6 +294,11 @@
         def _(m):
             unit(t, m, False)
 
+    def out_copy(t):
+        return pltpu.make_async_copy(out.at[t], out_hbm.at[t], out_sem.at[t])
+
+    load_hw.wait()
+
     def l1_edges(t, go):
         edges(l1box.at[t], 2, l1box.at[t], 2, lambda k: l1_send.at[t, k], 0,
               lambda k: l1_recv.at[t, k], 0, layer, go)
@@ -315,6 +331,10 @@
     def _(t):
         edges_arrived(l2box.at[t], 4, lambda k: l2_recv.at[t, k], 0)
         out[t] = (resid[t] + conv(l2box[t], hw[2], 4)).astype(BF16)
+        out_copy(t).start()
+
+    for t in range(steps):
+        out_copy(t).wait()
 
     @pl.loop(0, steps)
     def _(t):
@@ -342,17 +362,22 @@
     ch = enc_weight.shape[1]
     cells = rows * cols
     slots = steps * sections
-    vmem = pl.BlockSpec(memory_space=pltpu.VMEM)
     hbm = pl.BlockSpec(memory_space=pl.ANY)
     dma = pltpu.SemaphoreType.DMA
     rounded = pl.pallas_call(
         functools.partial(kernel, sections, spaces),
         out_shape=jax.ShapeDtypeStruct((steps, cells, ch), BF16),
-        in_specs=[hbm, vmem, vmem, vmem, hbm, vmem, vmem],
-        out_specs=vmem,
+        in_specs=[hbm] * 7,
+        out_specs=hbm,
         scratch_shapes=[
             pltpu.VMEM((steps, rows, 2, fine_cols, ch_in), BF16),
+            pltpu.VMEM(patch_weight.shape, BF16),
+            pltpu.VMEM((1, ch), F32),
+            pltpu.VMEM(enc_weight.shape, BF16),
             pltpu.VMEM(cell_weight.shape[1:], BF16),
+            pltpu.VMEM(cell_bias.shape, F32),
+            pltpu.VMEM(head_weight.shape, BF16),
+            pltpu.VMEM((steps, cells, ch), BF16),
             pltpu.VMEM((steps, cells, ch), BF16),
             pltpu.VMEM((steps, rows + 2, cols, ch), BF16),
             pltpu.VMEM((steps, rows, cols, ch), BF16),
@@ -364,13 +389,13 @@
             pltpu.VMEM((sections, cells, ch), F32),
             pltpu.VMEM((steps, cells, ch), F32),
             pltpu.VMEM((rows + 2, cols, 6 * ch), BF16),
-            dma((steps,)), dma((1,)),
+            dma((steps,)), dma((6,)), dma((steps,)),
             dma((steps, 2)), dma((steps, 2)), dma((steps, 3)),
             dma((slots, 3)), dma((slots, 2)), dma((slots, 5)), dma((steps, 3)),
             dma((steps, 2)), dma((steps, 2)), dma((steps, 2)), dma((steps, 2)),
         ],
         compiler_params=pltpu.CompilerParams(
-            collective_id=0, has_side_effects=True, vmem_limit_bytes=48 * 1024 * 1024
+            collective_id=0, has_side_effects=True, vmem_limit_bytes=56 * 1024 * 1024
         ),
         name="nowcast",
     )(

time: 71.1 us -> 64.3 us (0.904)
  local copies, waits for them, and re-layouts: 7.48 us -> 0.01 us
  matrix products: 1.7 us -> 2.69 us
    unnamed x18 -> x4, local copies, waits for them, and re-layouts: 7.48 us -> 0.01 us
    dot_general x1, matrix products: 1.7 us -> 2.69 us  [local(): jnp.dot(rounded.reshape(steps * cells, ch), out_weight, preferred_element...]
where the time goes in v1:
time: 64.3 us; the launch traced here: 64.1 us
  Pallas kernels  61.4 us (95%)
  matrix products  2.69 us (4%)
    pallas_call x1, Pallas kernels, local(): pl.pallas_call(functools.partial(kernel, sections, spaces), out_shape=jax...  61.4 us
    dot_general x1, matrix products, local(): jnp.dot(rounded.reshape(steps * cells, ch), out_weight, preferred_element...  2.69 us

profile of v1, /device:TPU:11, one launch (start us, length us, event | category | flops | bytes accessed | tf_op | source)
XLA Modules:
  0.0 64.1 jit_solution(3438936703178907083)
XLA Ops:
  0.0 0.0 copy-start
  0.0 0.0 copy-start.1
  0.0 61.4 %nowcast.1 = bf16[4,384,128]{2,1,0:T(8,128)(2,1)} custom-call(bf16[4,8,2,96,128]{4,3,2,1,0:T(8,128)(2,1)} %bitcast.8, bf16[2,256,128]{2,1,0:T(8,128)(2,1)} %pw_hbm.1, f32[1,128]{1,0:T(1,128)} %bitcast.10, bf16[1152,128]{1,0:T(8,128)(2,1)} %ew_hbm.1, bf16[2304,512]{1,0:T(8,128)(2,1)} %bitcast.7, f32[1,512]{1,0:T(1,128)} %cb_hbm.1, bf16[3,1152,128]{2,1,0:T(8,128)(2,1)} %hw_hbm.1), custom_call_target="tpu_custom_call" | custom-call | tf_op jit(solution)/shard_map/nowcast/pallas_call | solution.py:367
  61.4 0.0 copy-done
  61.4 0.0 copy-done.1
  61.4 2.7 %fusion = bf16[1536,512]{1,0:T(8,128)(2,1)} fusion(bf16[1536,128]{1,0:T(8,128)(2,1)} %bitcast.9, bf16[128,512]{1,0:T(8,128)(2,1)S(1)} %copy-done, f32[512]{0:T(512)S(1)} %copy-done.1), kind=kOutput, calls=%fused_computation.1 | convolution fusion | flops 202899456 | bytes 2099200 | tf_op jit(solution)/shard_map/dot_general | solution.py:410
Async XLA Ops:
  0.0 61.4 %copy-start = (bf16[128,512]{1,0:T(8,128)(2,1)S(1)}, bf16[128,512]{1,0:T(8,128)(2,1)}, u32[]{:S(2)}) copy-start(bf16[128,512]{1,0:T(8,128)(2,1)} %param.16) | copy-start | bytes 393220
  0.0 61.4 %copy-start.1 = (f32[512]{0:T(512)S(1)}, f32[512]{0:T(512)}, u32[]{:S(2)}) copy-start(f32[512]{0:T(512)} %param.17) | copy-start | bytes 6148

commit v2 on v1

--- a/solution.py
+++ b/solution.py
@@ -199,6 +199,7 @@
 
     load_cw.wait()
     load_cb.wait()
+    load_hw.wait()
 
     def h_edges(slot, go):
         edges(hbox.at[slot], 1, hbox.at[slot], 1, lambda k: u_send.at[slot, k], 0,
@@ -284,20 +285,8 @@
 
         outgoing(t, m, start)
 
-    @pl.loop(0, sections)
-    def _(m):
-        unit(0, m, True)
-
-    @pl.loop(1, steps)
-    def _(t):
-        @pl.loop(0, sections)
-        def _(m):
-            unit(t, m, False)
-
     def out_copy(t):
         return pltpu.make_async_copy(out.at[t], out_hbm.at[t], out_sem.at[t])
-
-    load_hw.wait()
 
     def l1_edges(t, go):
         edges(l1box.at[t], 2, l1box.at[t], 2, lambda k: l1_send.at[t, k], 0,
@@ -309,8 +298,7 @@
 
     zero = jnp.zeros((), BF16)
 
-    @pl.loop(0, steps)
-    def _(t):
+    def head_first(t):
         arrived(gbox.at[t, pl.ds(1, rows)], g_recv.at[t, 2])
         edges_arrived(gbox.at[t], 1, lambda k: g_recv.at[t, k], 0)
         base = gbox[t, pl.ds(1, rows)].reshape(cells, ch).astype(F32)
@@ -319,19 +307,40 @@
         l1box[t, pl.ds(2, rows)] = jnp.maximum(y, 0.0).astype(BF16).reshape(rows, cols, ch)
         l1_edges(t, start)
 
-    @pl.loop(0, steps)
-    def _(t):
+    def head_second(t):
         edges_arrived(l1box.at[t], 2, lambda k: l1_recv.at[t, k], 0)
         y = resid[t] + conv(l1box[t], hw[1], 2)
         resid[t] = y
         l2box[t, pl.ds(4, rows)] = jnp.maximum(y, 0.0).astype(BF16).reshape(rows, cols, ch)
         l2_edges(t, start)
 
-    @pl.loop(0, steps)
-    def _(t):
+    def head_third(t):
         edges_arrived(l2box.at[t], 4, lambda k: l2_recv.at[t, k], 0)
         out[t] = (resid[t] + conv(l2box[t], hw[2], 4)).astype(BF16)
         out_copy(t).start()
+
+    @pl.loop(0, sections)
+    def _(m):
+        unit(0, m, True)
+
+    @pl.loop(1, steps)
+    def _(t):
+        @pl.loop(0, sections)
+        def _(m):
+            unit(t, m, False)
+
+            for at, stage in ((1, head_first), (2, head_second), (3, head_third)):
+                @pl.when(jnp.logical_and(layer == last, m == min(at, sections - 1)))
+                def _():
+                    stage(t - 1)
+
+    @pl.loop(0, steps)
+    def _(t):
+        @pl.when(jnp.logical_or(layer != last, t == steps - 1))
+        def _():
+            head_first(t)
+            head_second(t)
+            head_third(t)
 
     for t in range(steps):
         out_copy(t).wait()

time: 64.3 us -> 81.4 us (1.27)
  the two profiles are of different devices: /device:TPU:11 before, /device:TPU:2 now
where the time goes in v2:
time: 81.4 us; the launch traced here: 81.3 us
  Pallas kernels  78.5 us (96%)
  matrix products  2.69 us (3%)
    pallas_call x1, Pallas kernels, local(): pl.pallas_call(functools.partial(kernel, sections, spaces), out_shape=jax...  78.5 us
    dot_general x1, matrix products, local(): jnp.dot(rounded.reshape(steps * cells, ch), out_weight, preferred_element...  2.69 us

profile of v2, /device:TPU:2, one launch (start us, length us, event | category | flops | bytes accessed | tf_op | source)
XLA Modules:
  0.0 81.3 jit_solution(11505009505996202963)
XLA Ops:
  0.0 0.0 copy-start
  0.0 0.0 copy-start.1
  0.0 78.5 %nowcast.1 = bf16[4,384,128]{2,1,0:T(8,128)(2,1)} custom-call(bf16[4,8,2,96,128]{4,3,2,1,0:T(8,128)(2,1)} %bitcast.8, bf16[2,256,128]{2,1,0:T(8,128)(2,1)} %pw_hbm.1, f32[1,128]{1,0:T(1,128)} %bitcast.10, bf16[1152,128]{1,0:T(8,128)(2,1)} %ew_hbm.1, bf16[2304,512]{1,0:T(8,128)(2,1)} %bitcast.7, f32[1,512]{1,0:T(1,128)} %cb_hbm.1, bf16[3,1152,128]{2,1,0:T(8,128)(2,1)} %hw_hbm.1), custom_call_target="tpu_custom_call" | custom-call | tf_op jit(solution)/shard_map/nowcast/pallas_call | solution.py:376
  78.6 0.0 copy-done
  78.6 0.0 copy-done.1
  78.6 2.7 %fusion = bf16[1536,512]{1,0:T(8,128)(2,1)} fusion(bf16[1536,128]{1,0:T(8,128)(2,1)} %bitcast.9, bf16[128,512]{1,0:T(8,128)(2,1)S(1)} %copy-done, f32[512]{0:T(512)S(1)} %copy-done.1), kind=kOutput, calls=%fused_computation.1 | convolution fusion | flops 202899456 | bytes 2099200 | tf_op jit(solution)/shard_map/dot_general | solution.py:419
Async XLA Ops:
  0.0 78.6 %copy-start = (bf16[128,512]{1,0:T(8,128)(2,1)S(1)}, bf16[128,512]{1,0:T(8,128)(2,1)}, u32[]{:S(2)}) copy-start(bf16[128,512]{1,0:T(8,128)(2,1)} %param.16) | copy-start | bytes 393220
  0.0 78.6 %copy-start.1 = (f32[512]{0:T(512)S(1)}, f32[512]{0:T(512)}, u32[]{:S(2)}) copy-start(f32[512]{0:T(512)} %param.17) | copy-start | bytes 6148

commit v3 on v1

--- a/solution.py
+++ b/solution.py
@@ -180,8 +180,7 @@
         slot = t * sections + layer
         return send(enc.at[t], xbox.at[slot, pl.ds(1, rows)], enc_send.at[t, 2], x_recv.at[slot, 2], 0, place)
 
-    @pl.loop(0, steps)
-    def _(t):
+    def encode(t):
         edges_arrived(ebox.at[t], 1, lambda k: e_recv.at[t, k], 0)
         result = proj[t].astype(F32) + conv(ebox[t], ew[...], 1)
         enc[t] = result.astype(BF16).reshape(rows, cols, ch)
@@ -197,8 +196,17 @@
 
         enc_out(t, start)
 
+    encode(0)
+
+    @pl.loop(1, steps)
+    def _(t):
+        @pl.when(layer != 0)
+        def _():
+            encode(t)
+
     load_cw.wait()
     load_cb.wait()
+    early = min(1, sections - 1)
 
     def h_edges(slot, go):
         edges(hbox.at[slot], 1, hbox.at[slot], 1, lambda k: u_send.at[slot, k], 0,
@@ -288,11 +296,19 @@
     def _(m):
         unit(0, m, True)
 
+        @pl.when(jnp.logical_and(layer == 0, m == early))
+        def _():
+            encode(1)
+
     @pl.loop(1, steps)
     def _(t):
         @pl.loop(0, sections)
         def _(m):
             unit(t, m, False)
+
+            @pl.when(jnp.logical_and(layer == 0, jnp.logical_and(m == early, t < steps - 1)))
+            def _():
+                encode(t + 1)
 
     def out_copy(t):
         return pltpu.make_async_copy(out.at[t], out_hbm.at[t], out_sem.at[t])

time: 64.3 us -> 66.4 us (1.033)
  Pallas kernels: 61.4 us -> 63.5 us
    pallas_call x1, Pallas kernels: 61.4 us -> 63.5 us  [local(): pl.pallas_call(functools.partial(kernel, sections, spaces), out_shape=jax...]
where the time goes in v3:
time: 66.4 us; the launch traced here: 66.3 us
  Pallas kernels  63.5 us (96%)
  matrix products  2.69 us (4%)
    pallas_call x1, Pallas kernels, local(): pl.pallas_call(functools.partial(kernel, sections, spaces), out_shape=jax...  63.5 us
    dot_general x1, matrix products, local(): jnp.dot(rounded.reshape(steps * cells, ch), out_weight, preferred_element...  2.69 us

profile of v3, /device:TPU:11, one launch (start us, length us, event | category | flops | bytes accessed | tf_op | source)
XLA Modules:
  0.0 66.3 jit_solution(9615362260418341304)
XLA Ops:
  0.0 0.0 copy-start
  0.0 0.0 copy-start.1
  0.0 63.5 %nowcast.1 = bf16[4,384,128]{2,1,0:T(8,128)(2,1)} custom-call(bf16[4,8,2,96,128]{4,3,2,1,0:T(8,128)(2,1)} %bitcast.8, bf16[2,256,128]{2,1,0:T(8,128)(2,1)} %pw_hbm.1, f32[1,128]{1,0:T(1,128)} %bitcast.10, bf16[1152,128]{1,0:T(8,128)(2,1)} %ew_hbm.1, bf16[2304,512]{1,0:T(8,128)(2,1)} %bitcast.7, f32[1,512]{1,0:T(1,128)} %cb_hbm.1, bf16[3,1152,128]{2,1,0:T(8,128)(2,1)} %hw_hbm.1), custom_call_target="tpu_custom_call" | custom-call | tf_op jit(solution)/shard_map/nowcast/pallas_call | solution.py:383
  63.6 0.0 copy-done
  63.6 0.0 copy-done.1
  63.6 2.7 %fusion = bf16[1536,512]{1,0:T(8,128)(2,1)} fusion(bf16[1536,128]{1,0:T(8,128)(2,1)} %bitcast.9, bf16[128,512]{1,0:T(8,128)(2,1)S(1)} %copy-done, f32[512]{0:T(512)S(1)} %copy-done.1), kind=kOutput, calls=%fused_computation.1 | convolution fusion | flops 202899456 | bytes 2099200 | tf_op jit(solution)/shard_map/dot_general | solution.py:426
Async XLA Ops:
  0.0 63.6 %copy-start = (bf16[128,512]{1,0:T(8,128)(2,1)S(1)}, bf16[128,512]{1,0:T(8,128)(2,1)}, u32[]{:S(2)}) copy-start(bf16[128,512]{1,0:T(8,128)(2,1)} %param.16) | copy-start | bytes 393220
  0.0 63.6 %copy-start.1 = (f32[512]{0:T(512)S(1)}, f32[512]{0:T(512)}, u32[]{:S(2)}) copy-start(f32[512]{0:T(512)} %param.17) | copy-start | bytes 6148

commit v4 on v1

--- a/solution.py
+++ b/solution.py
@@ -186,6 +186,7 @@
         result = proj[t].astype(F32) + conv(ebox[t], ew[...], 1)
         enc[t] = result.astype(BF16).reshape(rows, cols, ch)
         slot = t * sections + layer
+        enc_out(t, start)
 
         @pl.when(layer == 0)
         def _():
@@ -194,8 +195,6 @@
         @pl.when(layer != 0)
         def _():
             enc_main(t).start()
-
-        enc_out(t, start)
 
     load_cw.wait()
     load_cb.wait()
@@ -225,10 +224,14 @@
     def outgoing(t, m, go):
         slot = t * sections + m
 
+        @pl.when(t < steps - 1)
+        def _():
+            h_edges(slot, go)
+
         @pl.when(layer < last)
         def _():
+            x_edges(slot, go)
             go(x_main(slot))
-            x_edges(slot, go)
 
         @pl.when(layer == last)
         def _():
@@ -237,10 +240,6 @@
                 go(g_main(t, m))
 
             g_edges(t, m, go)
-
-        @pl.when(t < steps - 1)
-        def _():
-            h_edges(slot, go)
 
     def unit(t, m, first):
         slot = t * sections + m

time: 64.3 us -> 65.1 us (1.012)
  Pallas kernels: 61.4 us -> 62.2 us
    pallas_call x1, Pallas kernels: 61.4 us -> 62.2 us  [local(): pl.pallas_call(functools.partial(kernel, sections, spaces), out_shape=jax...]
where the time goes in v4:
time: 65.1 us; the launch traced here: 64.9 us
  Pallas kernels  62.2 us (96%)
  matrix products  2.7 us (4%)
    pallas_call x1, Pallas kernels, local(): pl.pallas_call(functools.partial(kernel, sections, spaces), out_shape=jax...  62.2 us
    dot_general x1, matrix products, local(): jnp.dot(rounded.reshape(steps * cells, ch), out_weight, preferred_element...  2.7 us

profile of v4, /device:TPU:11, one launch (start us, length us, event | category | flops | bytes accessed | tf_op | source)
XLA Modules:
  0.0 64.9 jit_solution(8160286874421306478)
XLA Ops:
  0.0 0.0 copy-start
  0.0 0.0 copy-start.1
  0.0 62.2 %nowcast.1 = bf16[4,384,128]{2,1,0:T(8,128)(2,1)} custom-call(bf16[4,8,2,96,128]{4,3,2,1,0:T(8,128)(2,1)} %bitcast.8, bf16[2,256,128]{2,1,0:T(8,128)(2,1)} %pw_hbm.1, f32[1,128]{1,0:T(1,128)} %bitcast.10, bf16[1152,128]{1,0:T(8,128)(2,1)} %ew_hbm.1, bf16[2304,512]{1,0:T(8,128)(2,1)} %bitcast.7, f32[1,512]{1,0:T(1,128)} %cb_hbm.1, bf16[3,1152,128]{2,1,0:T(8,128)(2,1)} %hw_hbm.1), custom_call_target="tpu_custom_call" | custom-call | tf_op jit(solution)/shard_map/nowcast/pallas_call | solution.py:366
  62.2 0.0 copy-done
  62.2 0.0 copy-done.1
  62.2 2.7 %fusion = bf16[1536,512]{1,0:T(8,128)(2,1)} fusion(bf16[1536,128]{1,0:T(8,128)(2,1)} %bitcast.9, bf16[128,512]{1,0:T(8,128)(2,1)S(1)} %copy-done, f32[512]{0:T(512)S(1)} %copy-done.1), kind=kOutput, calls=%fused_computation.1 | convolution fusion | flops 202899456 | bytes 2099200 | tf_op jit(solution)/shard_map/dot_general | solution.py:409
Async XLA Ops:
  0.0 62.2 %copy-start = (bf16[128,512]{1,0:T(8,128)(2,1)S(1)}, bf16[128,512]{1,0:T(8,128)(2,1)}, u32[]{:S(2)}) copy-start(bf16[128,512]{1,0:T(8,128)(2,1)} %param.16) | copy-start | bytes 393220
  0.0 62.2 %copy-start.1 = (f32[512]{0:T(512)S(1)}, f32[512]{0:T(512)}, u32[]{:S(2)}) copy-start(f32[512]{0:T(512)} %param.17) | copy-start | bytes 6148
